TPU v7x, 512 devices: a whole 4x4x16 slice. The times are simulated.
512 devices in a mesh: req: 32 (over z, core), seq: 16 (over y, x).
Axes of the slice: x: 4, y: 4, z: 16, core: 2. Of those that a mesh axis runs over, the one named last changes fastest.
Arguments:
- queries: bfloat16 [2, 32, 8192], P(None, 'req'), may hold values from -150 to 150
- kv_cache: bfloat16 [32, 12288, 2048], P('req', 'seq'), may hold values from -6 to 6
- context_length: int32 [32], P('req'), may hold values from 1 to 12288, as said below
- block_count: int32 [32], P('req'), may hold values from 1 to 128, as said below
- anchor_codes: int32 [32, 128, 2048], P(None, 'req', 'seq'), may hold values from -64 to 63
- delta_codes: int32 [32, 128, 16, 2048], P(None, 'req', None, 'seq'), may hold values from -64 to 63
- block_scale: float32 [32, 128, 2048], P(None, 'req', 'seq'), may hold values from 0.008 to 0.03
Outputs:
- attended: bfloat16 [2, 32, 8192], P(None, 'req', 'seq')
Inputs may be any that keep to these rules, and one draw needn't show every extreme that they name: Some request has context_length 12288. Some request has block_count 128.
All inputs are finite; a program needn't handle non-finite values.
Results may differ from a plain program's by a relative error of at most 0.0075.
Values may be sent and summed in bfloat16 or wider, within the bound.
A program may use at most 64 MiB of HBM per device.

v0:
```python
import jax
import jax.numpy as jnp
from jax import lax
from jax.sharding import PartitionSpec as P

H = 64
KVH = 8
HD = 128


def merged(value, axis, combine):
    everything = jax.tree.map(lambda part: lax.all_gather(part, axis), value)
    initial = jax.tree.map(lambda part: part[0], everything)

    def hop(k, so_far):
        return combine(so_far, jax.tree.map(lambda part: part[k], everything))

    return lax.fori_loop(1, lax.axis_size(axis), hop, initial)


def attend_part(queries, keys_values, visible):
    requests = keys_values.shape[0]
    groups = H // KVH
    query_heads = queries.reshape(queries.shape[0], requests, KVH, groups, HD)
    key_block = keys_values[:, :, : KVH * HD].reshape(requests, -1, KVH, HD)
    value_block = keys_values[:, :, KVH * HD :].reshape(requests, -1, KVH, HD)
    scores = jnp.einsum(
        "sbkgd,bnkd->sbkgn", query_heads, key_block, preferred_element_type=jnp.float32
    ) * HD ** (-0.5)
    shown = visible[None, :, None, None, :]
    scores = jnp.where(shown, scores, jnp.float32(-1e30))
    highest = jnp.max(scores, axis=-1)
    weights = jnp.where(shown, jnp.exp(scores - highest[..., None]), jnp.float32(0.0))
    totals = jnp.sum(weights, axis=-1)
    summed = jnp.einsum(
        "sbkgn,bnkd->sbkgd",
        weights.astype(jnp.bfloat16),
        value_block,
        preferred_element_type=jnp.float32,
    )
    return (highest, totals, summed)


def combine_parts(left_part, right_part):
    left_top, left_total, left_sum = left_part
    right_top, right_total, right_sum = right_part
    highest = jnp.maximum(left_top, right_top)
    left_weight = jnp.exp(left_top - highest)
    right_weight = jnp.exp(right_top - highest)
    totals = left_total * left_weight + right_total * right_weight
    summed = left_sum * left_weight[..., None] + right_sum * right_weight[..., None]
    return (highest, totals, summed)


def shards(queries, kv_cache, context_length, block_count, anchor_codes, delta_codes, block_scale):
    shard_count = lax.axis_size("seq")
    shard_index = lax.axis_index("seq")
    decoded = (
        block_scale[:, :, None, :] * (anchor_codes[:, :, None, :] + delta_codes).astype(jnp.float32)
    ).astype(jnp.bfloat16)
    arrived = lax.all_to_all(
        lax.all_to_all(decoded, "req", split_axis=0, concat_axis=1, tiled=True),
        "seq",
        split_axis=1,
        concat_axis=3,
        tiled=True,
    )
    local_blocks = arrived.shape[1]
    block_index = shard_index * local_blocks + jnp.arange(local_blocks, dtype=jnp.int32)
    requests, block_slots, block_rows, channels = arrived.shape
    block_live = block_index[None, :, None] < block_count[:, None, None]
    block_live = jnp.broadcast_to(block_live, (requests, block_slots, block_rows)).reshape(
        requests, block_slots * block_rows
    )
    arrived_rows = arrived.reshape(requests, block_slots * block_rows, channels)
    cached_count = kv_cache.shape[1]
    positions = shard_index * cached_count + jnp.arange(cached_count, dtype=jnp.int32)
    cached_live = positions[None, :] < context_length[:, None]
    cached_part = attend_part(queries, kv_cache, cached_live)
    arrived_part = attend_part(queries, arrived_rows, block_live)
    highest, totals, summed = combine_parts(cached_part, arrived_part)
    step_count = queries.shape[0]
    own_heads = H // shard_count
    highest, totals, summed = merged((highest, totals, summed), "seq", combine_parts)
    totals = totals.reshape(step_count, requests, H)
    summed = summed.reshape(step_count, requests, H, HD)
    first_head = shard_index * own_heads
    totals = lax.dynamic_slice_in_dim(totals, first_head, own_heads, 2)
    summed = lax.dynamic_slice_in_dim(summed, first_head, own_heads, 2)
    result = summed / totals[..., None]
    return result.reshape(step_count, requests, own_heads * HD).astype(jnp.bfloat16)


def solution(mesh):
    placed = (
        P(None, "req", None),
        P("req", "seq", None),
        P("req"),
        P("req"),
        P(None, "req", "seq"),
        P(None, "req", None, "seq"),
        P(None, "req", "seq"),
    )
    return jax.shard_map(
        shards, mesh=mesh, in_specs=placed, out_specs=P(None, "req", "seq"), check_vma=False
    )
```

profile of v0, /device:TPU:1, one launch (start us, length us, event | category | flops | bytes accessed | tf_op | source)
XLA Modules:
  0.0 151.6 jit_solution(15617755629136414648)
XLA Ops:
  6.5 2.3 %multiply_convert_fusion = bf16[32,4,16,128]{3,2,1,0:T(8,128)(2,1)} fusion(s32[32,4,16,128]{3,2,1,0:T(8,128)} %param.14, s32[32,4,128]{2,1,0:T(4,128)} %param.13, f32[32,4,128]{2,1,0:T(4,128)} %param.15), kind=kLoop, calls=%fused_computation.25 | loop fusion | flops 1048576 | bytes 1703936 | tf_op jit(solution)/shard_map/convert_element_type | solution.py:60
  8.8 16.8 %all-to-all-start = ((bf16[32,4,16,128]{3,2,1,0:T(8,128)(2,1)}), bf16[32,4,16,128]{3,2,1,0:T(8,128)(2,1)}, u32[]{:S(2)}, u32[]{:S(2)}) async-start(bf16[32,4,16,128]{3,2,1,0:T(8,128)(2,1)} %multiply_convert_fusion), calls=%async_computation | async-start | bytes 1048576 | tf_op jit(solution)/shard_map/all_to_all | solution.py:62
  26.3 3.3 %fusion.41 = (bf16[1,768,1024]{2,1,0:T(8,128)(2,1)S(1)}, bf16[1,768,1024]{2,1,0:T(8,128)(2,1)}) fusion(bf16[1,768,2048]{2,1,0:T(8,128)(2,1)} %param.10), kind=kLoop, calls=%fused_computation.66 | loop fusion | bytes 6291456 | tf_op jit(solution)/shard_map/slice | solution.py:26
  29.6 1.7 %copy.85 = bf16[1,768,1024]{1,2,0:T(8,128)(2,1)S(1)} copy(bf16[1,768,1024]{2,1,0:T(8,128)(2,1)} %get-tuple-element.231) | data formatting | bytes 3145728
  32.0 27.2 %all-to-all-done = bf16[32,4,16,128]{3,2,1,0:T(8,128)(2,1)} async-done(((bf16[32,4,16,128]{3,2,1,0:T(8,128)(2,1)}), bf16[32,4,16,128]{3,2,1,0:T(8,128)(2,1)}, u32[]{:S(2)}, u32[]{:S(2)}) %all-to-all-start) | async-done | bytes 524320 | tf_op jit(solution)/shard_map/all_to_all | solution.py:62
  59.2 6.8 %all-to-all-start.1 = ((bf16[1,128,16,128]{3,2,0,1:T(8,128)(2,1)}), bf16[1,128,16,128]{3,2,0,1:T(8,128)(2,1)}, u32[]{:S(2)}, u32[]{:S(2)}) async-start(bf16[1,128,16,128]{3,2,0,1:T(8,128)(2,1)} %bitcast.12), calls=%async_computation.1 | async-start | bytes 1048576 | tf_op jit(solution)/shard_map/all_to_all | solution.py:61
  66.2 1.6 %copy.86 = bf16[1,768,1024]{1,2,0:T(8,128)(2,1)} copy(bf16[1,768,1024]{2,1,0:T(8,128)(2,1)S(1)} %get-tuple-element.230) | data formatting | bytes 3145728
  67.8 1.2 fusion.44
  68.9 7.7 %all-to-all-done.1 = bf16[1,128,16,128]{3,2,0,1:T(8,128)(2,1)} async-done(((bf16[1,128,16,128]{3,2,0,1:T(8,128)(2,1)}), bf16[1,128,16,128]{3,2,0,1:T(8,128)(2,1)}, u32[]{:S(2)}, u32[]{:S(2)}) %all-to-all-start.1) | async-done | bytes 524320 | tf_op jit(solution)/shard_map/all_to_all | solution.py:61
  76.6 1.4 copy.53
  79.7 1.2 fusion.11
  81.3 16.5 %all_gather.15 = f32[16,2,1,8,8]{4,3,2,1,0:T(8,128)S(1)} all-gather(f32[1,2,1,8,8]{4,3,2,1,0:T(8,128)S(1)} %get-tuple-element.236), channel_id=1, replica_groups=mesh['req'=32,'seq'=16] {'seq'}, dimensions={0}, use_global_device_ids=true | all-gather | bytes 8704 | tf_op jit(solution)/shard_map/all_gather | solution.py:12
  97.8 17.9 %all_gather.14 = f32[16,2,1,8,8]{4,3,2,1,0:T(8,128)S(1)} all-gather(f32[1,2,1,8,8]{4,3,2,1,0:T(8,128)S(1)} %get-tuple-element.237), channel_id=1, replica_groups=mesh['req'=32,'seq'=16] {'seq'}, dimensions={0}, use_global_device_ids=true | all-gather | bytes 8704 | tf_op jit(solution)/shard_map/all_gather | solution.py:12
  115.7 11.7 %all-gather.3.cloned.1.call-done = f32[32,1,8,8,128]{4,3,0,2,1:T(8,128)} async-done(((f32[2,1,8,8,128]{4,3,0,2,1:T(8,128)}), f32[32,1,8,8,128]{4,3,0,2,1:T(8,128)}) %all-gather.3.cloned.1.call-update) | async-done | bytes 1048592 | tf_op jit(solution)/shard_map/all_gather | solution.py:12
  128.2 15.7 %while.19 = (s32[]{:T(128)}, f32[2,1,8,8]{3,2,0,1:T(8,128)S(1)}, f32[2,1,8,8]{3,2,0,1:T(8,128)S(1)}, f32[2,1,8,8,128]{4,3,2,1,0:T(8,128)S(1)}, f32[16,2,1,8,8]{4...) while((s32[]{:T(128)}, f32[2,1,8,8]{3,2,0,1:T(8,128)S(1)}, ...), condition=%wide.region_5.6_spmd, body=%wide.region_4.5_spmd.sunk | while | flops 50053 | bytes 204443 | solution.py:18
  128.3 1.0 fusion.54
  129.4 1.0 fusion.54
  130.4 1.0 fusion.54
  131.4 1.0 fusion.54
  132.5 1.0 fusion.54
  133.5 1.0 fusion.54
  134.6 1.0 fusion.54
  135.6 1.0 fusion.54
  139.8 1.0 fusion.54
  (79 shorter events, 10.2 us)
Async XLA Ops:
  8.8 50.4 %all-to-all-start = ((bf16[32,4,16,128]{3,2,1,0:T(8,128)(2,1)}), bf16[32,4,16,128]{3,2,1,0:T(8,128)(2,1)}, u32[]{:S(2)}, u32[]{:S(2)}) async-start(bf16[32,4,16,128]{3,2,1,0:T(8,128)(2,1)} %multiply_convert_fusion), calls=%async_computation | async-start | bytes 1048576 | tf_op jit(solution)/shard_map/all_to_all | solution.py:62
  59.2 17.5 %all-to-all-start.1 = ((bf16[1,128,16,128]{3,2,0,1:T(8,128)(2,1)}), bf16[1,128,16,128]{3,2,0,1:T(8,128)(2,1)}, u32[]{:S(2)}, u32[]{:S(2)}) async-start(bf16[1,128,16,128]{3,2,0,1:T(8,128)(2,1)} %bitcast.12), calls=%async_computation.1 | async-start | bytes 1048576 | tf_op jit(solution)/shard_map/all_to_all | solution.py:61
  66.0 61.4 %all-gather.3.cloned.1.call-start = ((), (), s32[]{:S(2)}) async-start(), calls=%async_computation.2 | async-start | bytes 1114112 | tf_op jit(solution)/shard_map/all_gather | solution.py:12
  78.0 0.8 copy-start.1
  78.2 1.4 copy-start
Sparse Core Ops, SparseCore 0:
  81.0 46.3 all-gather.2
where the time goes:
time: 153 us; the launch traced here: 152 us
  waiting for transfers between devices  46.5 us (30%)
  blocking collectives  34.4 us (22%)
  starting transfers between devices  23.7 us (15%)
  other arithmetic  17.7 us (12%)
  between operations  14.8 us (10%)
  local copies, waits for them, and re-layouts  10.9 us (7%)
  matrix products  2.89 us (2%)
    all_gather x2, blocking collectives, merged(): everything = jax.tree.map(lambda part: lax.all_gather(part, axis), value)  34.4 us
    all_to_all x1, waiting for transfers between devices, shards(): lax.all_to_all(decoded, 'req', split_axis=0, concat_axis=1, tiled=True)  27.2 us
    all_to_all x1, starting transfers between devices, shards(): lax.all_to_all(decoded, 'req', split_axis=0, concat_axis=1, tiled=True)  16.8 us
    add x15, other arithmetic, combine_parts(): left_sum * left_weight[..., None] + right_sum * right_weight[..., None]  14.4 us
    all_gather x1, waiting for transfers between devices, merged(): everything = jax.tree.map(lambda part: lax.all_gather(part, axis), value)  11.7 us
    all_to_all x1, waiting for transfers between devices, shards(): lax.all_to_all(lax.all_to_all(decoded, 'req', split_axis=0, concat_axis=1...  7.67 us
    all_to_all x1, starting transfers between devices, shards(): lax.all_to_all(lax.all_to_all(decoded, 'req', split_axis=0, concat_axis=1...  6.81 us
    unnamed x6, local copies, waits for them, and re-layouts  3.73 us
  transfers between devices with their start and end apart: 3, of which 3 were waited for; matrix products, arithmetic and copies ran while one was open for 6% of the time, Pallas kernels for 0%

commit v1 on v0

v1 whole, which is shorter than its diff:
```python
import jax
import jax.numpy as jnp
from jax import lax
from jax.experimental import pallas as pl
from jax.experimental.pallas import tpu as pltpu
from jax.sharding import PartitionSpec as P

H = 64
KVH = 8
HD = 128
GROUP = H // KVH
STEPS = 2
ROWS = GROUP * STEPS
MESH = pl.DeviceIdType.MESH
F32 = jnp.float32
BF16 = jnp.bfloat16
NEG = -1e30


def packed(summed, highest, totals):
    lane = lax.broadcasted_iota(jnp.int32, (8, HD), 1)
    coarse = totals.astype(BF16).astype(F32)
    stats = jnp.where(lane < 32, highest, jnp.where(lane < 64, coarse, totals - coarse))
    return jnp.concatenate([summed, stats], axis=0).astype(BF16)


def partial_attention(query, keys, values, live):
    scores = lax.dot_general(
        query, keys, (((1,), (1,)), ((), ())), preferred_element_type=F32
    ) * HD ** (-0.5)
    scores = jnp.where(live, scores, NEG)
    highest = jnp.max(scores, axis=1, keepdims=True).astype(BF16).astype(F32)
    weights = jnp.where(live, jnp.exp(scores - highest), 0.0)
    totals = jnp.sum(weights, axis=1, keepdims=True)
    summed = jnp.dot(weights.astype(BF16), values, preferred_element_type=F32)
    return highest, totals, summed


def kernel(
    q_hbm, cache_hbm, length_hbm, count_hbm, anchor_hbm, delta_hbm, scale_hbm,
    out_ref,
    q_v, cache_v, length_s, count_s, anchor_v, delta_v, scale_v,
    decoded, kv, q_all, count_mine, count_all, cached_msg, arrived_msg, inbox,
    load_sem, own_sem, q_send, q_recv, c_send, c_recv, kv_send, kv_recv,
    part_send, late_send, in_recv,
):
    r, s = lax.axis_index("req"), lax.axis_index("seq")
    z, c = r // 2, lax.rem(r, 2)
    h, k = s // 8, lax.rem(s, 8)
    slots = cache_hbm.shape[0]

    def place(zz, cc, ss):
        return (2 * zz + cc, ss)

    kin = [(1, 0), (0, 1), (1, 1)]

    def kin_place(dc, dh):
        return place(z, lax.rem(c + dc, 2), lax.rem(s + 8 * dh, 16))

    barrier = pltpu.get_barrier_semaphore()
    for d in range(1, 16):
        pl.semaphore_signal(barrier, inc=1, device_id=place(lax.rem(z + d, 16), c, s), device_id_type=MESH)
        pl.semaphore_signal(barrier, inc=1, device_id=place(z, c, lax.rem(s + d, 16)), device_id_type=MESH)
    for dc, dh in ((1, 0), (1, 1)):
        pl.semaphore_signal(barrier, inc=1, device_id=kin_place(dc, dh), device_id_type=MESH)

    loads = [
        pltpu.make_async_copy(src, dst, load_sem.at[n])
        for n, (src, dst) in enumerate(
            (
                (q_hbm, q_v),
                (count_hbm, count_s),
                (anchor_hbm, anchor_v),
                (scale_hbm, scale_v),
                (delta_hbm, delta_v),
                (length_hbm, length_s),
                (cache_hbm, cache_v),
            )
        )
    ]
    for load in loads:
        load.start()
    for load in loads[:5]:
        load.wait()
    count_mine[...] = jnp.full(count_mine.shape, count_s[0], jnp.int32)

    def decode(i, carry):
        for hh in range(2):
            for cc in range(2):
                q = 4 * i + 2 * hh + cc
                for b in range(4):
                    codes = anchor_v[q, b : b + 1, :] + delta_v[q, b]
                    decoded[hh, cc, i, 16 * b : 16 * b + 16, :] = (
                        scale_v[q, b : b + 1, :] * codes.astype(F32)
                    ).astype(BF16)
        return carry

    lax.fori_loop(0, 8, decode, 0)

    pl.semaphore_wait(barrier, 32)

    asks = lax.rem(z, 2) == h
    my_query = q_v.at[pl.ds(pl.multiple_of(ROWS * k, ROWS), ROWS), :]
    sent = []
    for d in (8, 7, 9, 6, 10, 5, 11, 4, 12, 3, 13, 2, 14, 1, 15):
        to = place(lax.rem(z + d, 16), c, s)
        for src, dst, ssem, rsem in (
            (my_query, q_all.at[z // 2], q_send.at[d - 1], q_recv),
            (count_mine.at[0], count_all.at[z // 2], c_send.at[d - 1], c_recv),
        ):
            sent.append(
                pltpu.make_async_remote_copy(
                    src_ref=src, dst_ref=dst, send_sem=ssem, recv_sem=rsem, device_id=to, device_id_type=MESH
                )
            )

    @pl.when(asks)
    def _():
        for copy in sent:
            copy.start()
        pltpu.make_async_copy(my_query, q_all.at[z // 2], q_recv).start()
        pltpu.make_async_copy(count_mine.at[0], count_all.at[z // 2], c_recv).start()

    def landing(hh, cc):
        return kv.at[hh, :, pl.ds(pl.multiple_of(64 * cc, 64), 64), :]

    swaps = []
    for n, (dc, dh) in enumerate(kin):
        swaps.append(
            pltpu.make_async_remote_copy(
                src_ref=decoded.at[lax.rem(h + dh, 2), lax.rem(c + dc, 2)],
                dst_ref=landing(h, c),
                send_sem=kv_send.at[n],
                recv_sem=kv_recv.at[n],
                device_id=kin_place(dc, dh),
                device_id_type=MESH,
            )
        )
        swaps[-1].start()
    own = pltpu.make_async_copy(decoded.at[h, c], landing(h, c), own_sem)
    own.start()

    for load in loads[5:]:
        load.wait()
    cached_live = s * slots + lax.broadcasted_iota(jnp.int32, (1, slots), 1) < length_s[0]
    for head in range(KVH):
        highest, totals, summed = partial_attention(
            q_v[ROWS * head : ROWS * head + ROWS, :],
            cache_v[:, HD * head : HD * head + HD],
            cache_v[:, HD * (KVH + head) : HD * (KVH + head) + HD],
            cached_live,
        )
        for e in range(2):
            part = slice(8 * e, 8 * e + 8)
            cached_msg[2 * head + e] = packed(summed[part], highest[part], totals[part])
    spread = []
    for d in range(1, 16):
        to = lax.rem(s + d, 16)
        spread.append(
            pltpu.make_async_remote_copy(
                src_ref=cached_msg.at[to],
                dst_ref=inbox.at[s],
                send_sem=part_send.at[d - 1],
                recv_sem=in_recv,
                device_id=place(z, c, to),
                device_id_type=MESH,
            )
        )
        spread[-1].start()
    pltpu.make_async_copy(cached_msg.at[s], inbox.at[s], in_recv).start()

    pltpu.make_async_copy(q_all, q_all, q_recv).wait()
    pltpu.make_async_copy(count_all, count_all, c_recv).wait()
    own.wait()
    for swap in swaps:
        swap.wait_recv()
    block = 8 * z + lax.broadcasted_iota(jnp.int32, (1, HD), 1) // 16
    for i in range(8):
        highest, totals, summed = partial_attention(
            q_all[i], kv[0, i], kv[1, i], block < count_all[i]
        )
        for e in range(2):
            part = slice(8 * e, 8 * e + 8)
            arrived_msg[2 * i + e] = packed(summed[part], highest[part], totals[part])
    returns = []
    for i in range(8):
        for e in range(2):
            zz, ss = 2 * i + h, 2 * k + e
            here = jnp.logical_and(zz == z, ss == s)
            copy = pltpu.make_async_remote_copy(
                src_ref=arrived_msg.at[2 * i + e],
                dst_ref=inbox.at[16 + z],
                send_sem=late_send.at[2 * i + e],
                recv_sem=in_recv,
                device_id=place(zz, c, ss),
                device_id_type=MESH,
            )
            returns.append((here, copy))

            @pl.when(jnp.logical_not(here))
            def _():
                copy.start()

            @pl.when(here)
            def _():
                pltpu.make_async_copy(arrived_msg.at[2 * i + e], inbox.at[16 + z], in_recv).start()

    pltpu.make_async_copy(inbox, inbox, in_recv).wait()
    parts = inbox[...].astype(F32)
    stats = parts[:, 8:, :]
    shrink = jnp.exp(stats - jnp.max(stats, axis=0, keepdims=True))[:, :, 0:1]
    totals = jnp.sum(shrink * (stats[:, :, 32:33] + stats[:, :, 64:65]), axis=0)
    summed = jnp.sum(shrink * parts[:, :8, :], axis=0)
    out_ref[...] = (summed / totals).astype(BF16)

    @pl.when(asks)
    def _():
        for copy in sent:
            copy.wait_send()

    for copy in swaps + spread:
        copy.wait_send()
    for here, copy in returns:

        @pl.when(jnp.logical_not(here))
        def _():
            copy.wait_send()


def shards(queries, kv_cache, context_length, block_count, anchor_codes, delta_codes, block_scale):
    slots = kv_cache.shape[1]
    rows = queries.reshape(STEPS, H, HD).swapaxes(0, 1).reshape(STEPS * H, HD)
    out = pl.pallas_call(
        kernel,
        out_shape=jax.ShapeDtypeStruct((8, HD), BF16),
        in_specs=[pl.BlockSpec(memory_space=pltpu.HBM)] * 7,
        out_specs=pl.BlockSpec(memory_space=pltpu.VMEM),
        scratch_shapes=[
            pltpu.VMEM((STEPS * H, HD), BF16),
            pltpu.VMEM((slots, 2 * KVH * HD), BF16),
            pltpu.SMEM((1,), jnp.int32),
            pltpu.SMEM((1,), jnp.int32),
            pltpu.VMEM((32, 4, HD), jnp.int32),
            pltpu.VMEM((32, 4, 16, HD), jnp.int32),
            pltpu.VMEM((32, 4, HD), F32),
            pltpu.VMEM((2, 2, 8, 64, HD), BF16),
            pltpu.VMEM((2, 8, 128, HD), BF16),
            pltpu.VMEM((8, ROWS, HD), BF16),
            pltpu.VMEM((1, 1, HD), jnp.int32),
            pltpu.VMEM((8, 1, HD), jnp.int32),
            pltpu.VMEM((16, 16, HD), BF16),
            pltpu.VMEM((16, 16, HD), BF16),
            pltpu.VMEM((32, 16, HD), BF16),
            pltpu.SemaphoreType.DMA((7,)),
            pltpu.SemaphoreType.DMA,
            pltpu.SemaphoreType.DMA((15,)),
            pltpu.SemaphoreType.DMA,
            pltpu.SemaphoreType.DMA((15,)),
            pltpu.SemaphoreType.DMA,
            pltpu.SemaphoreType.DMA((3,)),
            pltpu.SemaphoreType.DMA((3,)),
            pltpu.SemaphoreType.DMA((15,)),
            pltpu.SemaphoreType.DMA((16,)),
            pltpu.SemaphoreType.DMA,
        ],
        compiler_params=pltpu.CompilerParams(
            collective_id=0, has_side_effects=True, vmem_limit_bytes=60 << 20
        ),
    )(rows, kv_cache[0], context_length, block_count, anchor_codes, delta_codes, block_scale)
    return out.reshape(4, STEPS, HD).swapaxes(0, 1).reshape(STEPS, 1, 4 * HD)


def solution(mesh):
    placed = (
        P(None, "req", None),
        P("req", "seq", None),
        P("req"),
        P("req"),
        P(None, "req", "seq"),
        P(None, "req", None, "seq"),
        P(None, "req", "seq"),
    )
    return jax.shard_map(
        shards, mesh=mesh, in_specs=placed, out_specs=P(None, "req", "seq"), check_vma=False
    )
```

time: 153 us -> 39.6 us (0.26)
  the two profiles are of different devices: /device:TPU:1 before, /device:TPU:9 now
where the time goes in v1:
time: 39.6 us; the launch traced here: 39.5 us
  Pallas kernels  36.9 us (93%)
  between operations  1.3 us (3%)
  local copies, waits for them, and re-layouts  1.26 us (3%)
    pallas_call x1, Pallas kernels, shards(): pl.pallas_call(kernel, out_shape=jax.ShapeDtypeStruct((8, HD), BF16), in_...  36.9 us
    unnamed x1, local copies, waits for them, and re-layouts  1.26 us

profile of v1, /device:TPU:9, one launch (start us, length us, event | category | flops | bytes accessed | tf_op | source)
XLA Modules:
  0.0 39.5 jit_solution(5565891911431553871)
XLA Ops:
  1.3 36.9 %shard_map.73 = bf16[8,128]{1,0:T(8,128)(2,1)} custom-call(bf16[128,128]{1,0:T(8,128)(2,1)} %bitcast.12, bf16[768,2048]{1,0:T(8,128)(2,1)} %bitcast.11, s32[1]{0:T(128)S(6)} %copy.11.length_hbm, s32[1]{0:T(128)S(6)} %copy.12.count_hbm, s32[32,4,128]{2,1,0:T(4,128)} %anchor_hbm.1, s32[32,4,16,128]{3,2,1,0:T(8,128)} %delta_hbm.1, f32[32,4,128]{2,1,0:T(4,128)} %scale_hbm.1), custom_call_target="tpu_custom_call" | custom-call | tf_op jit(solution)/shard_map/pallas_call | solution.py:233
  38.2 1.3 %copy.13 = bf16[2,1,512]{2,0,1:T(2,128)(2,1)} copy(bf16[2,1,512]{2,0,1:T(2,128)(2,1)} %bitcast.13) | data formatting | bytes 4096

commit v2 on v1

v2 whole, which is shorter than its diff:
```python
import jax
import jax.numpy as jnp
from jax import lax
from jax.experimental import pallas as pl
from jax.experimental.pallas import tpu as pltpu
from jax.sharding import PartitionSpec as P

H = 64
KVH = 8
HD = 128
GROUP = H // KVH
STEPS = 2
ROWS = GROUP * STEPS
MESH = pl.DeviceIdType.MESH
F32 = jnp.float32
BF16 = jnp.bfloat16
NEG = -1e30
UP = (4, 3, 2, 1)
DOWN = (6, 5, 4, 3, 2, 1)
ONWARD = (5, 4, 3, 2, 1)
PARTS = 4


def packed(summed, highest, totals):
    lane = lax.broadcasted_iota(jnp.int32, (8, HD), 1)
    coarse = totals.astype(BF16).astype(F32)
    stats = jnp.where(lane < 32, highest, jnp.where(lane < 64, coarse, totals - coarse))
    return jnp.concatenate([summed, stats], axis=0).astype(BF16)


def partial_attention(query, keys, values, live):
    scores = lax.dot_general(
        query, keys, (((1,), (1,)), ((), ())), preferred_element_type=F32
    ) * HD ** (-0.5)
    scores = jnp.where(live, scores, NEG)
    highest = jnp.max(scores, axis=1, keepdims=True).astype(BF16).astype(F32)
    weights = jnp.where(live, jnp.exp(scores - highest), 0.0)
    totals = jnp.sum(weights, axis=1, keepdims=True)
    summed = jnp.dot(weights.astype(BF16), values, preferred_element_type=F32)
    return highest, totals, summed


def kernel(
    q_hbm, cache_hbm, length_s, count_s, anchor_hbm, delta_hbm, scale_hbm,
    out_ref,
    q_v, cache_v, anchor_v, delta_v, scale_v,
    decoded, kv, q_all, count_mine, count_all, cached_msg, arrived_msg, inbox,
    load_sem, q_send, q_recv, c_send, c_recv, kv_send, kv_recv,
    part_send, late_send, in_recv,
):
    r, s = lax.axis_index("req"), lax.axis_index("seq")
    z, c = r // 2, lax.rem(r, 2)
    side, head = s // 8, lax.rem(s, 8)
    h, k = lax.rem(s, 2), s // 2
    slots = cache_hbm.shape[0]

    def place(zz, cc, ss):
        return (2 * zz + cc, ss)

    barrier = pltpu.get_barrier_semaphore()
    asks = lax.rem(z, 2) == h
    over = s + 1 - 2 * h

    def along(d):
        return lax.rem(z + d + 16, 16)

    def greet(zz, ss):
        pl.semaphore_signal(barrier, inc=1, device_id=place(zz, c, ss), device_id_type=MESH)

    for d in range(1, 16):
        greet(z, lax.rem(s + d, 16))

    for sd in range(2):
        pl.semaphore_signal(barrier, inc=1, device_id=place(z, 1 - c, k + 8 * sd), device_id_type=MESH)

    @pl.when(asks)
    def _():
        for d in (2, 4):
            greet(along(-d), s)
        for d in (2, 4, 6):
            greet(along(d), over)

    @pl.when(jnp.logical_not(asks))
    def _():
        for d in (1, 3, 5):
            greet(along(-d), s)
            greet(along(d), over)

    loads = [
        pltpu.make_async_copy(src, dst, load_sem.at[n])
        for n, (src, dst) in enumerate(
            (
                (q_hbm, q_v),
                (anchor_hbm, anchor_v),
                (scale_hbm, scale_v),
                (delta_hbm, delta_v),
                (cache_hbm, cache_v),
            )
        )
    ]
    for load in loads:
        load.start()
    for load in loads[:4]:
        load.wait()
    count_mine[...] = jnp.full(count_mine.shape, count_s[0], jnp.int32)

    def decode(i, carry):
        for hh in range(2):
            for cc in range(2):
                q = 4 * i + 2 * hh + cc
                for b in range(4):
                    codes = anchor_v[q, b : b + 1, :] + delta_v[q, b]
                    decoded[hh, cc, i, 16 * b : 16 * b + 16, :] = (
                        scale_v[q, b : b + 1, :] * codes.astype(F32)
                    ).astype(BF16)
        return carry

    lax.fori_loop(0, 8, decode, 0)

    def cached_rows():
        for load in loads[4:]:
            load.wait()
        live = s * slots + lax.broadcasted_iota(jnp.int32, (1, slots), 1) < length_s[0]
        for head in range(KVH):
            highest, totals, summed = partial_attention(
                q_v[ROWS * head : ROWS * head + ROWS, :],
                cache_v[:, HD * head : HD * head + HD],
                cache_v[:, HD * (KVH + head) : HD * (KVH + head) + HD],
                live,
            )
            for e in range(2):
                part = slice(8 * e, 8 * e + 8)
                cached_msg[2 * head + e] = packed(summed[part], highest[part], totals[part])

    @pl.when(z < 8)
    def _():
        cached_rows()

    pl.semaphore_wait(barrier, jnp.where(asks, 22, 23))

    my_query = q_v.at[pl.ds(pl.multiple_of(ROWS * k, ROWS), ROWS), :]

    def bring(query, count, queries, counts, n, to):
        return [
            pltpu.make_async_remote_copy(
                src_ref=src, dst_ref=dst, send_sem=ssem.at[n], recv_sem=rsem.at[n], device_id=to, device_id_type=MESH
            )
            for src, dst, ssem, rsem in (
                (query, queries, q_send, q_recv),
                (count, counts, c_send, c_recv),
            )
        ]

    def slot_of(zz):
        return q_all.at[zz // 2], count_all.at[zz // 2]

    def came(queries, counts, n):
        for ref, sem in ((queries, q_recv), (counts, c_recv)):
            pltpu.make_async_copy(ref, ref, sem.at[n]).wait()

    mine = (my_query, count_mine.at[0])
    up, down, onward = [], [], []
    for d in UP:
        up += bring(*mine, *slot_of(z), d, place(along(d), c, s))
    for d in DOWN:
        down += bring(*mine, *slot_of(z), 16 - d, place(along(-d), c, over))
    for d in ONWARD:
        onward += bring(*slot_of(along(-4)), *slot_of(along(-4)), 4 + d, place(along(d), c, s))

    @pl.when(asks)
    def _():
        for copy in up:
            copy.start()
        for src, dst, sem in zip(mine, slot_of(z), (q_recv, c_recv)):
            pltpu.make_async_copy(src, dst, sem.at[0]).start()

    @pl.when(jnp.logical_not(asks))
    def _():
        for copy in down:
            copy.start()

    def landing(sd, cc, part):
        rows = pl.ds(pl.multiple_of(64 * cc, 64), 64)
        return kv.at[sd, 2 * part : 2 * part + 2, rows, :]

    swaps = []
    for part in range(PARTS):
        for hh in range(2):
            for cc in range(2):
                src = decoded.at[hh, cc, 2 * part : 2 * part + 2]
                here = jnp.logical_and(s == 2 * head + hh, c == cc)
                arrives = kv_recv.at[side, c, part]
                copy = pltpu.make_async_remote_copy(
                    src_ref=src,
                    dst_ref=landing(side, c, part),
                    send_sem=kv_send.at[4 * part + 2 * hh + cc],
                    recv_sem=arrives,
                    device_id=place(z, cc, 2 * head + hh),
                    device_id_type=MESH,
                )
                swaps.append((here, copy))

                @pl.when(jnp.logical_not(here))
                def _():
                    copy.start()

                @pl.when(here)
                def _():
                    pltpu.make_async_copy(src, landing(side, c, part), arrives).start()

    @pl.when(z >= 8)
    def _():
        cached_rows()

    @pl.when(asks)
    def _():
        came(*slot_of(along(-4)), 4)
        for copy in onward:
            copy.start()

    spread = []
    for d in range(1, 16):
        to = lax.rem(s + d, 16)
        spread.append(
            pltpu.make_async_remote_copy(
                src_ref=cached_msg.at[to],
                dst_ref=inbox.at[s],
                send_sem=part_send.at[d - 1],
                recv_sem=in_recv,
                device_id=place(z, c, to),
                device_id_type=MESH,
            )
        )
        spread[-1].start()
    pltpu.make_async_copy(cached_msg.at[s], inbox.at[s], in_recv).start()

    block = 8 * z + lax.broadcasted_iota(jnp.int32, (1, HD), 1) // 16
    returns = []
    for i in range(8):
        if i % 2 == 0:
            for sd in range(2):
                for cc in range(2):
                    ref = landing(sd, cc, i // 2)
                    pltpu.make_async_copy(ref, ref, kv_recv.at[sd, cc, i // 2]).wait()
        zz = 2 * i + h
        d = along(-zz)

        @pl.when(d != 4)
        def _():
            came(q_all.at[i], count_all.at[i], d)

        highest, totals, summed = partial_attention(
            q_all[i], kv[0, i], kv[1, i], block < count_all[i]
        )
        for e in range(2):
            part = slice(8 * e, 8 * e + 8)
            arrived_msg[2 * i + e] = packed(summed[part], highest[part], totals[part])
            ss = 2 * k + e
            here = jnp.logical_and(zz == z, ss == s)
            copy = pltpu.make_async_remote_copy(
                src_ref=arrived_msg.at[2 * i + e],
                dst_ref=inbox.at[16 + z],
                send_sem=late_send.at[2 * i + e],
                recv_sem=in_recv,
                device_id=place(zz, c, ss),
                device_id_type=MESH,
            )
            returns.append((here, copy))

            @pl.when(jnp.logical_not(here))
            def _():
                copy.start()

            @pl.when(here)
            def _():
                pltpu.make_async_copy(arrived_msg.at[2 * i + e], inbox.at[16 + z], in_recv).start()

    pltpu.make_async_copy(inbox, inbox, in_recv).wait()
    parts = inbox[...].astype(F32)
    stats = parts[:, 8:, :]
    shrink = jnp.exp(stats - jnp.max(stats, axis=0, keepdims=True))[:, :, 0:1]
    totals = jnp.sum(shrink * (stats[:, :, 32:33] + stats[:, :, 64:65]), axis=0)
    summed = jnp.sum(shrink * parts[:, :8, :], axis=0)
    out_ref[...] = (summed / totals).astype(BF16)

    @pl.when(asks)
    def _():
        for copy in up + onward:
            copy.wait_send()

    @pl.when(jnp.logical_not(asks))
    def _():
        for copy in down:
            copy.wait_send()

    for copy in spread:
        copy.wait_send()
    for here, copy in swaps + returns:

        @pl.when(jnp.logical_not(here))
        def _():
            copy.wait_send()


def shards(queries, kv_cache, context_length, block_count, anchor_codes, delta_codes, block_scale):
    slots = kv_cache.shape[1]
    rows = queries.reshape(STEPS, H, HD).swapaxes(0, 1).reshape(STEPS * H, HD)
    out = pl.pallas_call(
        kernel,
        out_shape=jax.ShapeDtypeStruct((8, HD), BF16),
        in_specs=[pl.BlockSpec(memory_space=pltpu.HBM)] * 2
        + [pl.BlockSpec(memory_space=pltpu.SMEM)] * 2
        + [pl.BlockSpec(memory_space=pltpu.HBM)] * 3,
        out_specs=pl.BlockSpec(memory_space=pltpu.VMEM),
        scratch_shapes=[
            pltpu.VMEM((STEPS * H, HD), BF16),
            pltpu.VMEM((slots, 2 * KVH * HD), BF16),
            pltpu.VMEM((32, 4, HD), jnp.int32),
            pltpu.VMEM((32, 4, 16, HD), jnp.int32),
            pltpu.VMEM((32, 4, HD), F32),
            pltpu.VMEM((2, 2, 8, 64, HD), BF16),
            pltpu.VMEM((2, 8, 128, HD), BF16),
            pltpu.VMEM((8, ROWS, HD), BF16),
            pltpu.VMEM((1, 1, HD), jnp.int32),
            pltpu.VMEM((8, 1, HD), jnp.int32),
            pltpu.VMEM((16, 16, HD), BF16),
            pltpu.VMEM((16, 16, HD), BF16),
            pltpu.VMEM((32, 16, HD), BF16),
            pltpu.SemaphoreType.DMA((5,)),
            pltpu.SemaphoreType.DMA((16,)),
            pltpu.SemaphoreType.DMA((16,)),
            pltpu.SemaphoreType.DMA((16,)),
            pltpu.SemaphoreType.DMA((16,)),
            pltpu.SemaphoreType.DMA((16,)),
            pltpu.SemaphoreType.DMA((2, 2, PARTS)),
            pltpu.SemaphoreType.DMA((15,)),
            pltpu.SemaphoreType.DMA((16,)),
            pltpu.SemaphoreType.DMA,
        ],
        compiler_params=pltpu.CompilerParams(
            collective_id=0, has_side_effects=True, vmem_limit_bytes=56541184
        ),
    )(rows, kv_cache[0], context_length, block_count, anchor_codes, delta_codes, block_scale)
    return out.reshape(4, STEPS, HD).swapaxes(0, 1).reshape(STEPS, 1, 4 * HD)


def solution(mesh):
    placed = (
        P(None, "req", None),
        P("req", "seq", None),
        P("req"),
        P("req"),
        P(None, "req", "seq"),
        P(None, "req", None, "seq"),
        P(None, "req", "seq"),
    )
    return jax.shard_map(
        shards, mesh=mesh, in_specs=placed, out_specs=P(None, "req", "seq"), check_vma=False
    )
```

time: 39.6 us -> 31.9 us (0.81)
  the two profiles are of different devices: /device:TPU:9 before, /device:TPU:96 now
where the time goes in v2:
time: 31.9 us; the launch traced here: 31.8 us
  Pallas kernels  29.9 us (94%)
  between operations  1.3 us (4%)
  local copies, waits for them, and re-layouts  0.58 us (2%)
    pallas_call x1, Pallas kernels, shards(): pl.pallas_call(kernel, out_shape=jax.ShapeDtypeStruct((8, HD), BF16), in_...  29.9 us

profile of v2, /device:TPU:96, one launch (start us, length us, event | category | flops | bytes accessed | tf_op | source)
XLA Modules:
  0.0 31.8 jit_solution(17617502926987645948)
XLA Ops:
  1.3 29.9 %shard_map.73 = bf16[8,128]{1,0:T(8,128)(2,1)S(1)} custom-call(bf16[128,128]{1,0:T(8,128)(2,1)} %bitcast.13, bf16[768,2048]{1,0:T(8,128)(2,1)} %bitcast.12, s32[1]{0:T(128)S(6)} %copy.11.length_s, s32[1]{0:T(128)S(6)} %copy.12.count_s, s32[32,4,128]{2,1,0:T(4,128)} %anchor_hbm.1, s32[32,4,16,128]{3,2,1,0:T(8,128)} %delta_hbm.1, f32[32,4,128]{2,1,0:T(4,128)} %scale_hbm.1), custom_call_target="tpu_custom_call" | custom-call | tf_op jit(solution)/shard_map/pallas_call | solution.py:308
  31.2 0.6 %copy.13 = bf16[2,1,512]{2,0,1:T(2,128)(2,1)} copy(bf16[2,1,512]{2,0,1:T(2,128)(2,1)S(1)} %bitcast.11) | data formatting | bytes 4096

commit v3 on v2

v3 whole, which is shorter than its diff:
```python
import functools

import jax
import jax.numpy as jnp
from jax import lax
from jax.experimental import pallas as pl
from jax.experimental.pallas import tpu as pltpu
from jax.sharding import PartitionSpec as P

H = 64
KVH = 8
HD = 128
GROUP = H // KVH
STEPS = 2
ROWS = GROUP * STEPS
MESH = pl.DeviceIdType.MESH
F32 = jnp.float32
BF16 = jnp.bfloat16
NEG = -1e30
UP = (4, 3, 2, 1)
DOWN = (7, 6, 5, 4, 3, 2, 1)
ONWARD = (6, 5, 4, 3, 2, 1)


def goes_down(z, d):
    return z >= {7: 12, 6: 4}.get(d, 0)


def goes_on(z, d):
    if d == 6:
        return jnp.logical_and(z >= 4, z < 8)
    return z >= {5: 4}.get(d, 0)


PARTS = ((0, 2), (2, 4), (4, 8))


def packed(summed, highest, totals):
    lane = lax.broadcasted_iota(jnp.int32, (8, HD), 1)
    coarse = totals.astype(BF16).astype(F32)
    stats = jnp.where(lane < 32, highest, jnp.where(lane < 64, coarse, totals - coarse))
    return jnp.concatenate([summed, stats], axis=0).astype(BF16)


def partial_attention(query, keys, values, live):
    scores = lax.dot_general(
        query, keys, (((1,), (1,)), ((), ())), preferred_element_type=F32
    ) * HD ** (-0.5)
    scores = jnp.where(live, scores, NEG)
    highest = jnp.max(scores, axis=1, keepdims=True).astype(BF16).astype(F32)
    weights = jnp.where(live, jnp.exp(scores - highest), 0.0)
    totals = jnp.sum(weights, axis=1, keepdims=True)
    summed = jnp.dot(weights.astype(BF16), values, preferred_element_type=F32)
    return highest, totals, summed


def kernel(
    q_hbm, cache_hbm, length_s, count_s, anchor_hbm, delta_hbm, scale_hbm,
    out_ref,
    q_v, cache_v, anchor_v, delta_v, scale_v,
    decoded, kv, q_all, mine, cached_msg, arrived_msg, inbox,
    load_sem, q_send, q_recv, kv_send, kv_recv,
    part_send, late_send, in_recv,
):
    r, s = lax.axis_index("req"), lax.axis_index("seq")
    z, c = r // 2, lax.rem(r, 2)
    side, head = s // 8, lax.rem(s, 8)
    h, k = lax.rem(s, 2), s // 2
    slots = cache_hbm.shape[0]

    def place(zz, cc, ss):
        return (2 * zz + cc, ss)

    barrier = pltpu.get_barrier_semaphore()
    asks = lax.rem(z, 2) == h
    over = s + 1 - 2 * h

    def along(d):
        return lax.rem(z + d + 16, 16)

    def greet(zz, ss):
        pl.semaphore_signal(barrier, inc=1, device_id=place(zz, c, ss), device_id_type=MESH)

    def greet_senders(ups, downs):
        for d in ups:
            pl.when(goes_on(along(-d), d))(functools.partial(greet, along(-d), s))
        for d in downs:
            pl.when(goes_down(along(d), d))(functools.partial(greet, along(d), over))

    pl.when(asks)(functools.partial(greet_senders, (6, 4, 2), (6, 4, 2)))
    pl.when(jnp.logical_not(asks))(functools.partial(greet_senders, (5, 3, 1), (7, 5, 3, 1)))
    n_on = sum(goes_on(z, d).astype(jnp.int32) for d in ONWARD)
    n_down = sum(goes_down(z, d).astype(jnp.int32) for d in DOWN)
    greeted_by = 17 + jnp.where(asks, n_on, n_down)

    for sd in range(2):
        pl.semaphore_signal(barrier, inc=1, device_id=place(z, 1 - c, k + 8 * sd), device_id_type=MESH)
    for d in range(1, 16):
        greet(z, lax.rem(s + d, 16))

    loads = [
        pltpu.make_async_copy(src, dst, load_sem.at[n])
        for n, (src, dst) in enumerate(
            (
                (q_hbm, q_v),
                (anchor_hbm, anchor_v),
                (scale_hbm, scale_v),
                (delta_hbm, delta_v),
                (cache_hbm, cache_v),
            )
        )
    ]
    for load in loads:
        load.start()
    for load in loads[:4]:
        load.wait()
    mine[:ROWS] = q_v[pl.ds(pl.multiple_of(ROWS * k, ROWS), ROWS), :]
    mine[ROWS:] = jnp.full((16, HD), count_s[0], jnp.int32).astype(F32).astype(BF16)

    def decode(i, carry):
        for hh in range(2):
            for cc in range(2):
                q = 4 * i + 2 * hh + cc
                for b in range(4):
                    codes = anchor_v[q, b : b + 1, :] + delta_v[q, b]
                    decoded[hh, cc, i, 16 * b : 16 * b + 16, :] = (
                        scale_v[q, b : b + 1, :] * codes.astype(F32)
                    ).astype(BF16)
        return carry

    lax.fori_loop(0, 8, decode, 0)

    def cached_rows():
        for load in loads[4:]:
            load.wait()
        live = s * slots + lax.broadcasted_iota(jnp.int32, (1, slots), 1) < length_s[0]
        for head in range(KVH):
            highest, totals, summed = partial_attention(
                q_v[ROWS * head : ROWS * head + ROWS, :],
                cache_v[:, HD * head : HD * head + HD],
                cache_v[:, HD * (KVH + head) : HD * (KVH + head) + HD],
                live,
            )
            for e in range(2):
                part = slice(8 * e, 8 * e + 8)
                cached_msg[2 * head + e] = packed(summed[part], highest[part], totals[part])

    early = jnp.logical_and(z < 8, jnp.logical_or(r > 0, s > 0))

    @pl.when(early)
    def _():
        cached_rows()

    pl.semaphore_wait(barrier, greeted_by)

    def bring(asked, zz, to):
        return pltpu.make_async_remote_copy(
            src_ref=asked,
            dst_ref=q_all.at[zz // 2],
            send_sem=q_send,
            recv_sem=q_recv.at[zz // 2],
            device_id=to,
            device_id_type=MESH,
        )

    def came(i):
        pltpu.make_async_copy(q_all.at[i], q_all.at[i], q_recv.at[i]).wait()

    below = along(-4)
    up = [(d > 0, bring(mine, z, place(along(d), c, s))) for d in UP]
    down = [(goes_down(z, d), bring(mine, z, place(along(-d), c, over))) for d in DOWN]
    onward = [(goes_on(z, d), bring(q_all.at[below // 2], below, place(along(d), c, s))) for d in ONWARD]

    def each(conditional, act):
        for wanted, copy in conditional:
            pl.when(wanted)(functools.partial(act, copy))

    def start(copy):
        copy.start()

    @pl.when(asks)
    def _():
        each(up, start)
        pltpu.make_async_copy(mine, q_all.at[z // 2], q_recv.at[z // 2]).start()

    @pl.when(jnp.logical_not(asks))
    def _():
        each(down, start)

    def landing(sd, cc, part):
        first, last = PARTS[part]
        return kv.at[sd, first:last, pl.ds(pl.multiple_of(64 * cc, 64), 64), :]

    def swap(part):
        first, last = PARTS[part]
        for hh in range(2):
            for cc in range(2):
                src = decoded.at[hh, cc, first:last]
                here = jnp.logical_and(s == 2 * head + hh, c == cc)
                arrives = kv_recv.at[part]
                copy = pltpu.make_async_remote_copy(
                    src_ref=src,
                    dst_ref=landing(side, c, part),
                    send_sem=kv_send,
                    recv_sem=arrives,
                    device_id=place(z, cc, 2 * head + hh),
                    device_id_type=MESH,
                )

                @pl.when(jnp.logical_not(here))
                def _():
                    copy.start()

                @pl.when(here)
                def _():
                    pltpu.make_async_copy(src, landing(side, c, part), arrives).start()

    def pass_on():
        came(below // 2)
        each(onward, start)

    middle = jnp.logical_and(z >= 4, z < 8)
    swap(0)
    pl.when(jnp.logical_and(asks, middle))(pass_on)
    swap(1)
    swap(2)

    @pl.when(jnp.logical_not(early))
    def _():
        cached_rows()


    spread = []
    for d in range(1, 16):
        to = lax.rem(s + d, 16)
        spread.append(
            pltpu.make_async_remote_copy(
                src_ref=cached_msg.at[to],
                dst_ref=inbox.at[s],
                send_sem=part_send,
                recv_sem=in_recv.at[0],
                device_id=place(z, c, to),
                device_id_type=MESH,
            )
        )

    def send_cached():
        for copy in spread:
            copy.start()
        pltpu.make_async_copy(cached_msg.at[s], inbox.at[s], in_recv.at[0]).start()

    pl.when(early)(send_cached)
    block = (8 * z + lax.broadcasted_iota(jnp.int32, (1, HD), 1) // 16).astype(F32)
    for i in range(8):
        if i == 0:
            pl.when(jnp.logical_and(asks, jnp.logical_not(middle)))(pass_on)
        if i == 2:
            pl.when(jnp.logical_not(early))(send_cached)
        for part in range(len(PARTS)):
            if i == PARTS[part][0]:
                ref = kv.at[:, slice(*PARTS[part])]
                pltpu.make_async_copy(ref, ref, kv_recv.at[part]).wait()
        zz = 2 * i + h
        d = along(-zz)

        @pl.when(d != 4)
        def _():
            came(i)

        highest, totals, summed = partial_attention(
            q_all[i, :ROWS], kv[0, i], kv[1, i], block < q_all[i, ROWS : ROWS + 1].astype(F32)
        )
        for e in range(2):
            part = slice(8 * e, 8 * e + 8)
            arrived_msg[2 * i + e] = packed(summed[part], highest[part], totals[part])
            ss = 2 * k + e
            here = jnp.logical_and(zz == z, ss == s)
            copy = pltpu.make_async_remote_copy(
                src_ref=arrived_msg.at[2 * i + e],
                dst_ref=inbox.at[16 + z],
                send_sem=late_send,
                recv_sem=in_recv.at[1],
                device_id=place(zz, c, ss),
                device_id_type=MESH,
            )

            @pl.when(jnp.logical_not(here))
            def _():
                copy.start()

            @pl.when(here)
            def _():
                pltpu.make_async_copy(arrived_msg.at[2 * i + e], inbox.at[16 + z], in_recv.at[1]).start()

    def merged(first, last):
        parts = inbox[first:last].astype(F32)
        stats = parts[:, 8:, :]
        highest = jnp.max(stats, axis=0)
        shrink = jnp.exp(stats - highest)[:, :, 0:1]
        totals = jnp.sum(shrink * (stats[:, :, 32:33] + stats[:, :, 64:65]), axis=0)
        return highest[:, 0:1], totals, jnp.sum(shrink * parts[:, :8, :], axis=0)

    def wait_inbox(first, last, n):
        pltpu.make_async_copy(inbox.at[first:last], inbox.at[first:last], in_recv.at[n]).wait()

    wait_inbox(0, 16, 0)
    cached_highest, cached_totals, cached_summed = merged(0, 16)

    def left(ref, sem):
        pltpu.make_async_copy(ref, ref, sem).wait()

    for n in range(len(ONWARD) + 1):
        pl.when(jnp.logical_and(asks, n_on == n))(
            functools.partial(left, inbox.at[: 2 * (n + len(UP))], q_send)
        )
    for n in range(1, len(DOWN) + 1):
        pl.when(jnp.logical_and(jnp.logical_not(asks), n_down == n))(
            functools.partial(left, inbox.at[: 2 * n], q_send)
        )
    kept = jnp.logical_or(s == 0, s == 15)
    pl.when(kept)(functools.partial(left, delta_v.at[:12], kv_send))
    pl.when(jnp.logical_not(kept))(functools.partial(left, delta_v.at[:16], kv_send))
    left(inbox.at[:15], part_send)
    pl.when(asks)(functools.partial(left, inbox.at[:15], late_send))
    pl.when(jnp.logical_not(asks))(functools.partial(left, inbox.at[:16], late_send))

    wait_inbox(16, 32, 1)
    highest, totals, summed = merged(16, 32)
    top = jnp.maximum(highest, cached_highest)
    shrink, cached_shrink = jnp.exp(highest - top), jnp.exp(cached_highest - top)
    out_ref[...] = (
        (summed * shrink + cached_summed * cached_shrink)
        / (totals * shrink + cached_totals * cached_shrink)
    ).astype(BF16)


def shards(queries, kv_cache, context_length, block_count, anchor_codes, delta_codes, block_scale):
    slots = kv_cache.shape[1]
    rows = queries.reshape(STEPS, H, HD).swapaxes(0, 1).reshape(STEPS * H, HD)
    out = pl.pallas_call(
        kernel,
        out_shape=jax.ShapeDtypeStruct((8, HD), BF16),
        in_specs=[pl.BlockSpec(memory_space=pltpu.HBM)] * 2
        + [pl.BlockSpec(memory_space=pltpu.SMEM)] * 2
        + [pl.BlockSpec(memory_space=pltpu.HBM)] * 3,
        out_specs=pl.BlockSpec(memory_space=pltpu.VMEM),
        scratch_shapes=[
            pltpu.VMEM((STEPS * H, HD), BF16),
            pltpu.VMEM((slots, 2 * KVH * HD), BF16),
            pltpu.VMEM((32, 4, HD), jnp.int32),
            pltpu.VMEM((32, 4, 16, HD), jnp.int32),
            pltpu.VMEM((32, 4, HD), F32),
            pltpu.VMEM((2, 2, 8, 64, HD), BF16),
            pltpu.VMEM((2, 8, 128, HD), BF16),
            pltpu.VMEM((8, ROWS + 16, HD), BF16),
            pltpu.VMEM((ROWS + 16, HD), BF16),
            pltpu.VMEM((16, 16, HD), BF16),
            pltpu.VMEM((16, 16, HD), BF16),
            pltpu.VMEM((32, 16, HD), BF16),
            pltpu.SemaphoreType.DMA((5,)),
            pltpu.SemaphoreType.DMA,
            pltpu.SemaphoreType.DMA((8,)),
            pltpu.SemaphoreType.DMA,
            pltpu.SemaphoreType.DMA((len(PARTS),)),
            pltpu.SemaphoreType.DMA,
            pltpu.SemaphoreType.DMA,
            pltpu.SemaphoreType.DMA((2,)),
        ],
        compiler_params=pltpu.CompilerParams(
            collective_id=0, has_side_effects=True, vmem_limit_bytes=56541184
        ),
    )(rows, kv_cache[0], context_length, block_count, anchor_codes, delta_codes, block_scale)
    return out.reshape(4, STEPS, HD).swapaxes(0, 1).reshape(STEPS, 1, 4 * HD)


def solution(mesh):
    placed = (
        P(None, "req", None),
        P("req", "seq", None),
        P("req"),
        P("req"),
        P(None, "req", "seq"),
        P(None, "req", None, "seq"),
        P(None, "req", "seq"),
    )
    return jax.shard_map(
        shards, mesh=mesh, in_specs=placed, out_specs=P(None, "req", "seq"), check_vma=False
    )
```

time: 31.9 us -> 29.4 us (0.922)
  the two profiles are of different devices: /device:TPU:96 before, /device:TPU:1 now
where the time goes in v3:
time: 29.4 us; the launch traced here: 29.3 us
  Pallas kernels  27.4 us (93%)
  between operations  1.3 us (4%)
  local copies, waits for them, and re-layouts  0.58 us (2%)
    pallas_call x1, Pallas kernels, shards(): pl.pallas_call(kernel, out_shape=jax.ShapeDtypeStruct((8, HD), BF16), in_...  27.4 us

profile of v3, /device:TPU:1, one launch (start us, length us, event | category | flops | bytes accessed | tf_op | source)
XLA Modules:
  0.0 29.3 jit_solution(13688290451468041448)
XLA Ops:
  1.3 27.4 %shard_map.73 = bf16[8,128]{1,0:T(8,128)(2,1)S(1)} custom-call(bf16[128,128]{1,0:T(8,128)(2,1)} %bitcast.13, bf16[768,2048]{1,0:T(8,128)(2,1)} %bitcast.12, s32[1]{0:T(128)S(6)} %copy.11.length_s, s32[1]{0:T(128)S(6)} %copy.12.count_s, s32[32,4,128]{2,1,0:T(4,128)} %anchor_hbm.1, s32[32,4,16,128]{3,2,1,0:T(8,128)} %delta_hbm.1, f32[32,4,128]{2,1,0:T(4,128)} %scale_hbm.1), custom_call_target="tpu_custom_call" | custom-call | tf_op jit(solution)/shard_map/pallas_call | solution.py:340
  28.7 0.6 %copy.13 = bf16[2,1,512]{2,0,1:T(2,128)(2,1)} copy(bf16[2,1,512]{2,0,1:T(2,128)(2,1)S(1)} %bitcast.11) | data formatting | bytes 4096

commit v4 on v3

--- a/solution.py
+++ b/solution.py
@@ -268,7 +268,7 @@
             came(i)
 
         highest, totals, summed = partial_attention(
-            q_all[i, :ROWS], kv[0, i], kv[1, i], block < q_all[i, ROWS : ROWS + 1].astype(F32)
+            q_all[i, :ROWS], kv[0, i], kv[1, i], block < q_all[i, ROWS:].astype(F32)
         )
         for e in range(2):
             part = slice(8 * e, 8 * e + 8)

time: 29.4 us -> 29.4 us (level)
  no operation moved by 1% of the time
where the time goes in v4:
time: 29.4 us; the launch traced here: 29.3 us
  Pallas kernels  27.4 us (93%)
  between operations  1.3 us (4%)
  local copies, waits for them, and re-layouts  0.58 us (2%)
    pallas_call x1, Pallas kernels, shards(): pl.pallas_call(kernel, out_shape=jax.ShapeDtypeStruct((8, HD), BF16), in_...  27.4 us

profile of v4, /device:TPU:1, one launch (start us, length us, event | category | flops | bytes accessed | tf_op | source)
XLA Modules:
  0.0 29.3 jit_solution(15048433701871442543)
XLA Ops:
  1.3 27.4 %shard_map.73 = bf16[8,128]{1,0:T(8,128)(2,1)S(1)} custom-call(bf16[128,128]{1,0:T(8,128)(2,1)} %bitcast.13, bf16[768,2048]{1,0:T(8,128)(2,1)} %bitcast.12, s32[1]{0:T(128)S(6)} %copy.11.length_s, s32[1]{0:T(128)S(6)} %copy.12.count_s, s32[32,4,128]{2,1,0:T(4,128)} %anchor_hbm.1, s32[32,4,16,128]{3,2,1,0:T(8,128)} %delta_hbm.1, f32[32,4,128]{2,1,0:T(4,128)} %scale_hbm.1), custom_call_target="tpu_custom_call" | custom-call | tf_op jit(solution)/shard_map/pallas_call | solution.py:340
  28.7 0.6 %copy.13 = bf16[2,1,512]{2,0,1:T(2,128)(2,1)} copy(bf16[2,1,512]{2,0,1:T(2,128)(2,1)S(1)} %bitcast.11) | data formatting | bytes 4096
